TPU v7x, 512 devices: a whole 4x8x8 slice. The times are simulated.
512 devices in a mesh: rep: 16 (over y, x_hi), grp: 32 (over z, x_lo, core).
Axes of the slice: x: 4 (x_hi: 2, x_lo: 2; x = x_hi * 2 + x_lo), y: 8, z: 8, core: 2. Of those that a mesh axis runs over, the one named last changes fastest.
Arguments:
- grad_parts: bfloat16 [16, 2, 5120, 2048], P('rep', None, 'grp'), may hold values from -6 to 6
- master: float32 [2, 5120, 2048], P(None, 'grp', 'rep'), may hold values from -0.078125 to 0.078125
- first_moment: float32 [2, 5120, 2048], P(None, 'grp', 'rep'), may hold values from -2.4 to 2.4
- second_moment: float32 [2, 5120, 2048], P(None, 'grp', 'rep'), may hold values from 0.002 to 0.2
- actor_weights: bfloat16 [2, 2048, 5120], P(None, 'grp'), may hold values from -0.119628906 to 0.119628906
Outputs:
- new_actor: bfloat16 [2, 2048, 5120], P(None, 'grp')
- new_master: float32 [2, 5120, 2048], P(None, 'grp', 'rep')
- new_first: float32 [2, 5120, 2048], P(None, 'grp', 'rep')
- new_second: float32 [2, 5120, 2048], P(None, 'grp', 'rep')
All inputs are finite; a program needn't handle non-finite values.
Results may differ from a plain program's by a relative error of at most 0.014.
Values may be sent and summed in bfloat16 or wider, within the bound.
A program may use at most 64 MiB of HBM per device.

v0:
```python
import jax
import jax.numpy as jnp
from jax import lax
from jax.sharding import PartitionSpec as P

bias_one = 0.9999734386011124
bias_two = 0.09520785288629106
learn_rate = 0.01
decay_rate = 0.1


def adam_step(grad, master, first_moment, second_moment):
    new_first = 0.9 * first_moment + 0.1 * grad
    new_second = 0.999 * second_moment + 0.001 * grad * grad
    update = new_first / bias_one / (jnp.sqrt(new_second / bias_two) + 1e-08) + decay_rate * master
    new_master = master - learn_rate * update
    delta = (-learn_rate * update).astype(jnp.bfloat16)
    return (delta, new_master, new_first, new_second)


def body(grad_parts, master, first_moment, second_moment, actor_weights):
    local_grad = grad_parts[0].astype(jnp.float32)
    grad = lax.psum_scatter(
        local_grad.astype(jnp.bfloat16), "rep", scatter_dimension=2, tiled=True
    ).astype(jnp.float32)
    delta, new_master, new_first, new_second = adam_step(grad, master, first_moment, second_moment)
    full_rows = lax.all_gather(delta, "rep", axis=2, tiled=True)
    moved = lax.all_to_all(
        jnp.swapaxes(full_rows, 1, 2), "grp", split_axis=1, concat_axis=2, tiled=True
    )
    new_actor = (actor_weights.astype(jnp.float32) + moved.astype(jnp.float32)).astype(jnp.bfloat16)
    return (new_actor, new_master, new_first, new_second)


def solution(mesh):
    in_specs = (
        P("rep", None, "grp", None),
        P(None, "grp", "rep"),
        P(None, "grp", "rep"),
        P(None, "grp", "rep"),
        P(None, "grp", None),
    )
    out_specs = (
        P(None, "grp", None),
        P(None, "grp", "rep"),
        P(None, "grp", "rep"),
        P(None, "grp", "rep"),
    )
    return jax.shard_map(body, mesh=mesh, in_specs=in_specs, out_specs=out_specs, check_vma=False)
```

profile of v0, /device:TPU:6, one launch (start us, length us, event | category | flops | bytes accessed | tf_op | source)
XLA Modules:
  0.0 407.7 jit_solution(8776295832482892070)
XLA Ops:
  7.2 0.0 reduce-scatter.4.cloned.1.call-start
  7.2 4.7 %copy.17 = bf16[2,160,2048]{1,0,2:T(2,128)(2,1)S(1)} copy(bf16[2,160,2048]{2,1,0:T(8,128)(2,1)} %bitcast.11) | data formatting | bytes 2621440
  11.9 0.0 copy-start
  11.9 0.0 copy-start.3
  11.9 0.0 copy-start.4
  11.9 2.0 reshape.14
  13.9 0.0 reduce-scatter.4.cloned.1.call-update
  14.0 0.0 all-gather.2.cloned.1.call-start
  14.0 214.1 %reduce-scatter.4.cloned.1.call-done = bf16[128,320]{1,0:T(8,128)(2,1)} async-done(((bf16[2048,320]{1,0:T(8,128)(2,1)}), bf16[128,320]{1,0:T(8,128)(2,1)}) %reduce-scatter.4.cloned.1.call-update) | async-done | bytes 81936
  228.1 1.0 reshape.15
  229.1 0.1 copy.18
  229.2 0.0 copy-done
  229.2 0.0 copy-done.3
  229.2 0.0 copy-done.4
  229.2 0.8 multiply_subtract_fusion
  230.1 0.0 copy-start.1
  230.1 0.0 copy-start.2
  230.1 0.7 multiply_convert_fusion
  230.8 0.0 all-gather.2.cloned.1.call-update
  230.8 82.6 %all-gather.2.cloned.1.call-done = bf16[2,160,2048]{2,1,0:T(8,128)(2,1)} async-done(((bf16[2,160,128]{2,1,0:T(8,128)(2,1)}), bf16[2,160,2048]{2,1,0:T(8,128)(2,1)}) %all-gather.2.cloned.1.call-update) | async-done | bytes 1310736 | tf_op jit(solution)/shard_map/all_gather | solution.py:27
  313.4 4.7 %copy.14 = bf16[2,2048,160]{2,0,1:T(2,128)(2,1)S(1)} copy(bf16[2,2048,160]{1,2,0:T(8,128)(2,1)} %bitcast.12) | data formatting | bytes 2621440 | tf_op jit(solution)/shard_map/transpose | solution.py:29
  318.1 60.3 %all_to_all.4 = bf16[2,2048,160]{2,0,1:T(2,128)(2,1)} all-to-all(bf16[2,2048,160]{2,0,1:T(2,128)(2,1)S(1)} %copy.14), channel_id=1, replica_groups=mesh['rep'=16,'grp'=32] {'grp'}, dimensions={1} | all-to-all | bytes 2621440 | tf_op jit(solution)/shard_map/all_to_all | solution.py:28
  378.4 0.0 copy-done.1
  378.4 0.0 copy-done.2
  378.4 4.7 %copy.15 = bf16[2,2048,160]{1,2,0:T(8,128)(2,1)S(1)} copy(bf16[2,2048,160]{2,0,1:T(2,128)(2,1)} %all_to_all.4) | data formatting | bytes 2621440 | tf_op jit(solution)/shard_map/all_to_all | solution.py:28
  383.1 3.5 reshape.13
  386.6 7.1 %copy.16 = f32[2,64,32,160]{3,2,1,0:T(8,128)} copy(f32[2,64,32,160]{1,2,3,0:T(8,128)} %bitcast.9) | data formatting | bytes 5242880 | tf_op jit(solution)/shard_map/convert_element_type | solution.py:31
  393.7 4.6 %reshape.12 = f32[2,64,5120]{2,1,0:T(8,128)S(1)} reshape(f32[2,64,32,160]{3,2,1,0:T(8,128)} %copy.16) | data formatting | bytes 5242880 | tf_op jit(solution)/shard_map/convert_element_type | solution.py:31
  398.3 2.6 add_convert_fusion
Async XLA Ops:
  7.2 220.9 %reduce-scatter.4.cloned.1.call-start = ((), (), s32[]{:S(2)}) async-start(), calls=%async_computation.3 | async-start | bytes 1671168
  11.9 217.3 %copy-start = (f32[2,160,128]{2,1,0:T(8,128)S(1)}, f32[2,160,128]{2,1,0:T(8,128)}, u32[]{:S(2)}) copy-start(f32[2,160,128]{2,1,0:T(8,128)} %param.6) | copy-start | bytes 491524
  11.9 217.3 %copy-start.3 = (f32[2,160,128]{2,1,0:T(8,128)S(1)}, f32[2,160,128]{2,1,0:T(8,128)}, u32[]{:S(2)}) copy-start(f32[2,160,128]{2,1,0:T(8,128)} %param.7) | copy-start | bytes 491524
  11.9 217.3 %copy-start.4 = (f32[2,160,128]{2,1,0:T(8,128)S(1)}, f32[2,160,128]{2,1,0:T(8,128)}, u32[]{:S(2)}) copy-start(f32[2,160,128]{2,1,0:T(8,128)} %param.8) | copy-start | bytes 491524
  14.0 299.5 %all-gather.2.cloned.1.call-start = ((), (), s32[]{:S(2)}) async-start(), calls=%async_computation.2 | async-start | bytes 1392640 | tf_op jit(solution)/shard_map/all_gather | solution.py:27
  230.1 148.3 %copy-start.1 = (f32[2,160,128]{2,1,0:T(8,128)}, f32[2,160,128]{2,1,0:T(8,128)S(1)}, u32[]{:S(2)}) copy-start(f32[2,160,128]{2,1,0:T(8,128)S(1)} %get-tuple-element.5) | copy-start | bytes 491524
  230.1 148.3 %copy-start.2 = (f32[2,160,128]{2,1,0:T(8,128)}, f32[2,160,128]{2,1,0:T(8,128)S(1)}, u32[]{:S(2)}) copy-start(f32[2,160,128]{2,1,0:T(8,128)S(1)} %get-tuple-element.6) | copy-start | bytes 491524
Sparse Core Ops, SparseCore 0:
  14.1 213.9 reduce-scatter.3
  232.2 81.2 all-gather.1
where the time goes:
time: 409 us; the launch traced here: 408 us
  waiting for transfers between devices  297 us (73%)
  blocking collectives  60.3 us (15%)
  local copies, waits for them, and re-layouts  32.3 us (8%)
  between operations  14.1 us (3%)
  other arithmetic  4.18 us (1%)
    unnamed x3, waiting for transfers between devices  214 us
    all_gather x1, waiting for transfers between devices, body(): full_rows = lax.all_gather(delta, 'rep', axis=2, tiled=True)  82.6 us
    all_to_all x1, blocking collectives, body(): lax.all_to_all(jnp.swapaxes(full_rows, 1, 2), 'grp', split_axis=1, concat...  60.3 us
    convert_element_type x3, local copies, waits for them, and re-layouts, body(): moved.astype(jnp.float32)  15.2 us
  transfers between devices with their start and end apart: 2, of which 2 were waited for; matrix products, arithmetic and copies ran while one was open for 0% of the time, Pallas kernels for 0%

commit v1 on v0

v1 whole, which is shorter than its diff:
```python
import jax
import jax.numpy as jnp
from jax import lax
from jax.experimental import pallas as pl
from jax.experimental.pallas import tpu as pltpu
from jax.sharding import PartitionSpec as P

MESH = pl.DeviceIdType.MESH

bias_one = 0.9999734386011124
bias_two = 0.09520785288629106
learn_rate = 0.01
decay_rate = 0.1

NY = 8
LAYERS = 2
ROWS = 160
HALF = ROWS // 2
COLS = 128
PIECE = 16
SPAN = 640
Z_ORDER = (0, 4, 2, 6, 1, 5, 3, 7)
F32 = jnp.float32
BF16 = jnp.bfloat16


def kernel(
    grad, master, first, second, actor,
    new_actor, new_master, new_first, new_second,
    grad_v, master_v, first_v, second_v, actor_v,
    sum_recv, sum_send, one_recv, one_send, swapped, total, cross_send, cross_recv,
    padded, delta_send, delta_recv, piece,
    load_sem, store_sem, rs_send, rs_recv, swap_sems, cross_sems, move_send, move_recv, ag_send, ag_recv, ag_cross, ag_over, piece_sem,
):
    r, g = lax.axis_index("rep"), lax.axis_index("grp")
    y, h = r // 2, r % 2
    z, lo, core = g // 4, (g // 2) % 2, g % 2
    ring = (((y + 1) % NY) * 2 + h, ((y + NY - 1) % NY) * 2 + h)
    beyond = (((y + 2) % NY) * 2 + h, ((y + NY - 2) % NY) * 2 + h)
    partner = y * 2 + (1 - h)

    def at(dy):
        return (y + dy + 2 * NY) % NY

    def flip(bit, by):
        return (bit + by) % 2

    def remote(source, target, send_sem, recv_sem, rep, grp):
        return pltpu.make_async_remote_copy(
            src_ref=source, dst_ref=target, send_sem=send_sem, recv_sem=recv_sem,
            device_id={"rep": rep, "grp": grp}, device_id_type=MESH,
        )

    grad_load = pltpu.make_async_copy(grad.at[0], grad_v, load_sem.at[0])
    grad_load.start()
    unit = pl.ds(pl.multiple_of((y // 2) * PIECE, PIECE), PIECE)
    first_z = 2 * flip(h, core) + 1 - y % 2
    loads = [
        pltpu.make_async_copy(master, master_v, load_sem.at[1]),
        pltpu.make_async_copy(first, first_v, load_sem.at[2]),
        pltpu.make_async_copy(second, second_v, load_sem.at[3]),
    ]
    for t in range(2):
        rows = pl.ds(pl.multiple_of((first_z + 4 * t) * SPAN, 128), SPAN)
        loads.append(pltpu.make_async_copy(actor.at[:, unit, rows], actor_v.at[t], load_sem.at[4 + t]))
    for load in loads:
        load.start()

    def target(to, other):
        return (2 * to + 1 - z % 2) * 2 + flip((z // 2) % 2, other), 2 * r + other

    barrier = pltpu.get_barrier_semaphore()
    greeted = [(peer, g) for peer in (*ring, *beyond, partner)]
    greeted += [target(to, other) for to in range(4) for other in range(2)]
    greeted += [(2 * z + lo, 4 * (first_z + 4 * t) + j) for t in range(2) for j in range(4)]
    for rep, grp in greeted:
        pl.semaphore_signal(barrier, inc=1, device_id={"rep": rep, "grp": grp}, device_id_type=MESH)
    padded[...] = jnp.zeros_like(padded)
    pl.semaphore_wait(barrier, len(greeted))

    def dest_of(way, hops):
        return at(hops if way == 0 else -hops)

    def both(dest):
        return pl.ds(pl.multiple_of(dest * 2 * COLS, 2 * COLS), 2 * COLS)

    def one(dest, owner):
        return pl.ds(pl.multiple_of((dest * 2 + owner) * COLS, COLS), COLS)

    def rs_copy(way, hops, layer, half, own=False):
        rows = pl.ds(half * HALF, HALF)
        if layer == 1:
            source, place = one_send.at[way, hops - 1, rows], one_recv.at[way, hops - 1, rows]
        else:
            place = sum_recv.at[way, hops - 1, rows]
            source = grad_v.at[0, rows, both(dest_of(way, hops))] if own else sum_send.at[way, hops - 1, rows]
        return remote(
            source, place, rs_send.at[way, hops - 1, layer, half], rs_recv.at[way, hops - 1, layer, half],
            beyond[way] if hops == 4 else ring[way], g,
        )

    def swap(offset):
        return remote(
            grad_v.at[1, :, one(at(offset), 1 - h)], swapped.at[offset % NY],
            swap_sems.at[0, offset % NY], swap_sems.at[1, offset % NY], partner, g,
        )

    sent = []

    def start(copy):
        copy.start()
        sent.append(copy)

    def rows_of(half):
        return pl.ds(half * HALF, HALF)

    def with_swapped(offset, rows):
        return grad_v[1, rows, one(at(offset), h)].astype(F32) + swapped[offset % NY, rows, :].astype(F32)

    grad_load.wait()
    start(swap(4))
    for half in range(2):
        start(rs_copy(half, 4, 0, half, True))
        for way in range(2):
            start(rs_copy(way, 3, 0, half, True))
    for offset in (3, -3, 2, -2, 1, -1, 0):
        start(swap(offset))
    swap(4).wait_recv()
    for way in range(2):
        one_send[way, 3, rows_of(way), :] = with_swapped(4, rows_of(way)).astype(BF16)
        start(rs_copy(way, 4, 1, way))
    for way in range(2):
        swap(3 if way == 0 else -3).wait_recv()
        for half in range(2):
            one_send[way, 2, rows_of(half), :] = with_swapped(3 if way == 0 else -3, rows_of(half)).astype(BF16)
            start(rs_copy(way, 3, 1, half))
    for hops in (2, 1):
        for half in range(2):
            for way in range(2):
                rows = rows_of(half)
                rs_copy(way, hops + 1, 0, half, True).wait_recv()
                summed = grad_v[0, rows, both(dest_of(way, hops))].astype(F32)
                summed = summed + sum_recv[way, hops, rows, :].astype(F32)
                if hops == 2 and half == way:
                    rs_copy(way, 4, 0, half, True).wait_recv()
                    summed = summed + sum_recv[way, 3, rows, :].astype(F32)
                sum_send[way, hops - 1, rows, :] = summed.astype(BF16)
                start(rs_copy(way, hops, 0, half))
        for way in range(2):
            swap(hops if way == 0 else -hops).wait_recv()
        for half in range(2):
            for way in range(2):
                rows = rows_of(half)
                rs_copy(way, hops + 1, 1, half).wait_recv()
                summed = with_swapped(hops if way == 0 else -hops, rows) + one_recv[way, hops, rows, :].astype(F32)
                if hops == 2 and half == way:
                    rs_copy(way, 4, 1, half).wait_recv()
                    summed = summed + one_recv[way, 3, rows, :].astype(F32)
                one_send[way, hops - 1, rows, :] = summed.astype(BF16)
                start(rs_copy(way, hops, 1, half))

    def cross(half):
        rows = rows_of(half)
        return remote(
            cross_send.at[rows], cross_recv.at[rows], cross_sems.at[0, half], cross_sems.at[1, half], partner, g
        )

    for half in range(2):
        for way in range(2):
            rs_copy(way, 1, 0, half).wait_recv()
        rows = rows_of(half)

        def last(owner, rows=rows):
            side = pl.ds(pl.multiple_of(owner * COLS, COLS), COLS)
            summed = grad_v[0, rows, one(y, owner)].astype(F32)
            for way in range(2):
                summed = summed + sum_recv[way, 0, rows, side].astype(F32)
            return summed

        cross_send[rows, :] = last(1 - h).astype(BF16)
        start(cross(half))
        total[0, rows, :] = last(h)
    swap(0).wait_recv()
    for half in range(2):
        for way in range(2):
            rs_copy(way, 1, 1, half).wait_recv()
        rows = rows_of(half)
        summed = with_swapped(0, rows)
        for way in range(2):
            summed = summed + one_recv[way, 0, rows, :].astype(F32)
        total[1, rows, :] = summed

    for load in loads:
        load.wait()
    slot = (z // 4) * 4 + g % 4
    shift = pl.multiple_of((g % 4) * 32, 32)
    stores = []
    for layer in (1, 0):
        gradient = total[layer]
        if layer == 0:
            for half in range(2):
                cross(half).wait_recv()
            gradient = gradient + cross_recv[...].astype(F32)
        moment = 0.9 * first_v[layer] + 0.1 * gradient
        square = 0.999 * second_v[layer] + 0.001 * gradient * gradient
        weight = master_v[layer]
        update = moment * (1.0 / bias_one) / (jnp.sqrt(square * (1.0 / bias_two)) + 1e-08) + decay_rate * weight
        step = -learn_rate * update
        padded[layer, pl.ds(shift, ROWS), :] = step
        delta_send[layer] = padded[layer].T.astype(BF16)
        for to in range(4):
            for other in range(2):
                start(
                    remote(
                        delta_send.at[layer, pl.ds(other * 64 + to * PIECE, PIECE)], delta_recv.at[layer, slot],
                        move_send.at[layer, to, other], move_recv.at[layer], *target(to, other),
                    )
                )
        master_v[layer] = weight + step
        first_v[layer] = moment
        second_v[layer] = square
        for index, (array, result) in enumerate(
            ((master_v, new_master), (first_v, new_first), (second_v, new_second))
        ):
            store = pltpu.make_async_copy(array.at[layer], result.at[layer], store_sem.at[index, layer])
            store.start()
            stores.append(store)

    def region(origin, owner, layer, half=None):
        z_block = (1 - origin % 2) * 4 + flip(owner, core) * 2
        z_range = pl.ds(z_block, 2) if half is None else pl.ds(z_block + half, 1)
        return new_actor.at[layer, z_range, pl.ds(pl.multiple_of((origin // 2) * PIECE, PIECE), PIECE)]

    def ag_copy(way, hops, layer, other):
        owner = 1 - h if other else h
        held = 2 if hops == 4 else hops - 1
        place = region(at(-held if way == 0 else held), owner, layer, way if hops == 4 else None)
        source = piece.at[layer] if hops == 1 and not other else place
        return remote(
            source, place,
            ag_send.at[way, hops - 1, layer, other], ag_recv.at[way, hops - 1, layer, other],
            beyond[way] if hops == 4 else ring[way], g,
        )

    def ag_cross_copy(layer):
        return remote(
            piece.at[layer], region(y, h, layer), ag_cross.at[0, layer], ag_cross.at[1, layer], partner, g
        )

    for layer in (1, 0):
        pltpu.make_async_copy(delta_recv.at[layer], delta_recv.at[layer], move_recv.at[layer]).wait()
        for t in range(2):
            low = [delta_recv[layer, 4 * t + j, :, :128].astype(F32) for j in range(4)]
            high = [delta_recv[layer, 4 * t + j, :, 128:].astype(F32) for j in range(4)]
            tiles = [low[0], high[0] + low[1], high[1] + low[2], high[2] + low[3], high[3]]
            for index, tile in enumerate(tiles):
                place = slice(index * 128, index * 128 + 128)
                piece[layer, t, :, place] = (actor_v[t, layer, :, place].astype(F32) + tile).astype(BF16)
        for way in range(2):
            start(ag_copy(way, 1, layer, 0))
        if layer == 0:
            start(ag_cross_copy(0))
            start(ag_cross_copy(1))
        store = pltpu.make_async_copy(piece.at[layer], region(y, h, layer), piece_sem.at[layer])
        store.start()
        stores.append(store)

    def over(hops, way, other):
        place = region(at(-hops if way == 0 else hops), 1 - h if other else h, 1, way if hops == 4 else None)
        return remote(place, place, ag_over.at[0, way, hops - 1], ag_over.at[1, way, hops - 1], partner, g)

    def gather(hops, layer, other, last=False):
        for way in range(2):
            for come in (3, 4) if last else (hops,):
                if come == 0:
                    ag_cross_copy(layer).wait_recv() if way == 0 else None
                else:
                    ag_copy(way, come, layer, other).wait_recv()
                if come == 2:
                    start(ag_copy(way, 4, layer, other))
                if come < 3:
                    start(ag_copy(way, come + 1, layer, other))
                if layer == 1:
                    start(over(come, way, 0))

    gather(1, 1, 0)
    gather(1, 0, 0)
    gather(0, 0, 1)
    gather(2, 1, 0)
    gather(2, 0, 0)
    gather(1, 0, 1)
    gather(3, 1, 0, True)
    gather(2, 0, 1)
    gather(3, 0, 0, True)
    gather(3, 0, 1, True)
    ag_cross_copy(1).wait_recv()
    for hops in (1, 2, 3, 4):
        for way in range(2):
            over(hops, way, 1).wait_recv()

    for copy in sent:
        copy.wait_send()
    for store in stores:
        store.wait()


def place_kernel(actor, master, first, second, new_actor, new_master, new_first, new_second, sems):
    copies = [
        pltpu.make_async_copy(
            actor.at[:, index], new_actor.at[:, :, pl.ds(place * SPAN, SPAN)], sems.at[index]
        )
        for index, place in enumerate(Z_ORDER)
    ]
    for index, (array, result) in enumerate(((master, new_master), (first, new_first), (second, new_second))):
        copies.append(pltpu.make_async_copy(array, result, sems.at[NY + index]))
    for copy in copies:
        copy.start()
    for copy in copies:
        copy.wait()


def body(grad_parts, master, first_moment, second_moment, actor_weights):
    args = [
        pltpu.with_memory_space_constraint(array, pltpu.HBM)
        for array in (grad_parts, master, first_moment, second_moment, actor_weights)
    ]
    anywhere = pl.BlockSpec(memory_space=pl.ANY)
    state = jax.ShapeDtypeStruct(master.shape, F32)
    state_v = pltpu.VMEM((LAYERS, ROWS, COLS), F32)
    dma = pltpu.SemaphoreType.DMA
    results = pl.pallas_call(
        kernel,
        out_shape=(jax.ShapeDtypeStruct((LAYERS, NY, 64, SPAN), BF16), state, state, state),
        in_specs=[anywhere] * 5,
        out_specs=[anywhere] * 4,
        scratch_shapes=[
            pltpu.VMEM((LAYERS, ROWS, 2048), BF16),
            state_v,
            state_v,
            state_v,
            pltpu.VMEM((2, LAYERS, PIECE, SPAN), BF16),
            pltpu.VMEM((2, 4, ROWS, 2 * COLS), BF16),
            pltpu.VMEM((2, 2, ROWS, 2 * COLS), BF16),
            pltpu.VMEM((2, 4, ROWS, COLS), BF16),
            pltpu.VMEM((2, 4, ROWS, COLS), BF16),
            pltpu.VMEM((NY, ROWS, COLS), BF16),
            state_v,
            pltpu.VMEM((ROWS, COLS), BF16),
            pltpu.VMEM((ROWS, COLS), BF16),
            pltpu.VMEM((LAYERS, 256, COLS), F32),
            pltpu.VMEM((LAYERS, COLS, 256), BF16),
            pltpu.VMEM((LAYERS, 8, PIECE, 256), BF16),
            pltpu.VMEM((LAYERS, 2, PIECE, SPAN), BF16),
            dma((6,)),
            dma((3, LAYERS)),
            dma((2, 4, LAYERS, 2)),
            dma((2, 4, LAYERS, 2)),
            dma((2, NY)),
            dma((2, 2)),
            dma((LAYERS, 4, 2)),
            dma((LAYERS,)),
            dma((2, 4, LAYERS, 2)),
            dma((2, 4, LAYERS, 2)),
            dma((2, LAYERS)),
            dma((2, 2, 4)),
            dma((LAYERS,)),
        ],
        compiler_params=pltpu.CompilerParams(
            collective_id=0, has_side_effects=True, vmem_limit_bytes=48 * 1024 * 1024
        ),
    )(*args)
    return pl.pallas_call(
        place_kernel,
        out_shape=(jax.ShapeDtypeStruct(actor_weights.shape, BF16), state, state, state),
        in_specs=[anywhere] * 4,
        out_specs=[anywhere] * 4,
        scratch_shapes=[dma((NY + 3,))],
        compiler_params=pltpu.CompilerParams(vmem_limit_bytes=4 * 1024 * 1024),
    )(*results)


def solution(mesh):
    in_specs = (
        P("rep", None, "grp", None),
        P(None, "grp", "rep"),
        P(None, "grp", "rep"),
        P(None, "grp", "rep"),
        P(None, "grp", None),
    )
    out_specs = (
        P(None, "grp", None),
        P(None, "grp", "rep"),
        P(None, "grp", "rep"),
        P(None, "grp", "rep"),
    )
    return jax.shard_map(body, mesh=mesh, in_specs=in_specs, out_specs=out_specs, check_vma=False)
```

time: 409 us -> 60.7 us (0.15)
  waiting for transfers between devices: 297 us -> 0 us
  blocking collectives: 60.3 us -> 0 us
  Pallas kernels: 0 us -> 59 us
  local copies, waits for them, and re-layouts: 32.3 us -> 0 us
  between operations: 14.1 us -> 0.64 us
  other arithmetic: 4.18 us -> 0 us
    unnamed x3 -> x0, waiting for transfers between devices: 214 us -> none
    all_gather x1 -> x0, waiting for transfers between devices: 82.6 us -> none  [body(): full_rows = lax.all_gather(delta, 'rep', axis=2, tiled=True)]
    all_to_all x1 -> x0, blocking collectives: 60.3 us -> none  [body(): lax.all_to_all(jnp.swapaxes(full_rows, 1, 2), 'grp', split_axis=1, concat...]
    pallas_call x0 -> x2, Pallas kernels: none -> 59 us  [the longest x1 57.7 us: body(): pl.pallas_call(kernel, out_shape=(jax.ShapeDtypeStruct((LAYERS, NY, 64, S...]
    convert_element_type x3 -> x0, local copies, waits for them, and re-layouts: 15.2 us -> none  [body(): moved.astype(jnp.float32)]
    unnamed x14 -> x0, local copies, waits for them, and re-layouts: 7.83 us -> none
    all_to_all x1 -> x0, local copies, waits for them, and re-layouts: 4.66 us -> none  [body(): lax.all_to_all(jnp.swapaxes(full_rows, 1, 2), 'grp', split_axis=1, concat...]
    transpose x1 -> x0, local copies, waits for them, and re-layouts: 4.66 us -> none  [body(): jnp.swapaxes(full_rows, 1, 2)]
  transfers between devices with their start and end apart: 2 -> 0, of which waited for: 2 -> 0; matrix products, arithmetic and copies ran while one was open for 0% -> 0% of each run, Pallas kernels for 0% -> 0%
where the time goes in v1:
time: 60.7 us; the launch traced here: 59.6 us
  Pallas kernels  59 us (97%)
  between operations  0.64 us (1%)
    pallas_call x1, Pallas kernels, body(): pl.pallas_call(kernel, out_shape=(jax.ShapeDtypeStruct((LAYERS, NY, 64, S...  57.7 us
    pallas_call x1, Pallas kernels, body(): pl.pallas_call(place_kernel, out_shape=(jax.ShapeDtypeStruct(actor_weight...  1.31 us

profile of v1, /device:TPU:6, one launch (start us, length us, event | category | flops | bytes accessed | tf_op | source)
XLA Modules:
  0.0 59.6 jit_solution(18040376874483565936)
XLA Ops:
  0.6 57.7 %shard_map.84 = (bf16[2,8,64,640]{3,2,1,0:T(8,128)(2,1)S(1)}, f32[2,160,128]{2,1,0:T(8,128)S(1)}, f32[2,160,128]{2,1,0:T(8,128)S(1)}, f32[2,160,128]{2,1,0:T(8,128)S(1)}) custom-call(bf16[1,2,160,2048]{3,2,1,0:T(8,128)(2,1)} %grad.1, f32[2,160,128]{2,1,0:T(8,128)} %master.1, f32[2,160,128]{2,1,0:T(8,128)} %first.1, f32[2,160,128]{2,1,0:T(8,128)} %second.1, ...), custom_call_target="tpu_custom_call" | custom-call | tf_op jit(solution)/shard_map/pallas_call | solution.py:331
  58.3 1.3 %shard_map.85 = (bf16[2,64,5120]{2,1,0:T(8,128)(2,1)}, f32[2,160,128]{2,1,0:T(8,128)}, f32[2,160,128]{2,1,0:T(8,128)}, f32[2,160,128]{2,1,0:T(8,128)}) custom-call(bf16[2,8,64,640]{3,2,1,0:T(8,128)(2,1)S(1)} %get-tuple-element.8.actor, f32[2,160,128]{2,1,0:T(8,128)S(1)} %get-tuple-element.9.master, f32[2,160,128]{2,1,0:T(8,128)S(1)} %get-tuple-element.10.first, ...), custom_call_target="tpu_custom_call" | custom-call | tf_op jit(solution)/shard_map/pallas_call | solution.py:372

commit v2 on v1

--- a/solution.py
+++ b/solution.py
@@ -28,15 +28,16 @@
     grad, master, first, second, actor,
     new_actor, new_master, new_first, new_second,
     grad_v, master_v, first_v, second_v, actor_v,
-    sum_recv, sum_send, one_recv, one_send, swapped, total, cross_send, cross_recv,
+    sum_recv, sum_send, last_recv, raw_recv, one_recv, one_send, swapped, total,
     padded, delta_send, delta_recv, piece,
-    load_sem, store_sem, rs_send, rs_recv, swap_sems, cross_sems, move_send, move_recv, ag_send, ag_recv, ag_cross, ag_over, piece_sem,
+    load_sem, store_sem, rs_send, rs_recv, last_sems, raw_sems, swap_sems, move_send, move_recv, ag_send, ag_recv, ag_cross, ag_over, piece_sem,
 ):
     r, g = lax.axis_index("rep"), lax.axis_index("grp")
     y, h = r // 2, r % 2
     z, lo, core = g // 4, (g // 2) % 2, g % 2
     ring = (((y + 1) % NY) * 2 + h, ((y + NY - 1) % NY) * 2 + h)
     beyond = (((y + 2) % NY) * 2 + h, ((y + NY - 2) % NY) * 2 + h)
+    across = (((y + 1) % NY) * 2 + 1 - h, ((y + NY - 1) % NY) * 2 + 1 - h)
     partner = y * 2 + (1 - h)
 
     def at(dy):
@@ -70,7 +71,7 @@
         return (2 * to + 1 - z % 2) * 2 + flip((z // 2) % 2, other), 2 * r + other
 
     barrier = pltpu.get_barrier_semaphore()
-    greeted = [(peer, g) for peer in (*ring, *beyond, partner)]
+    greeted = [(peer, g) for peer in (*ring, *beyond, *across, partner)]
     greeted += [target(to, other) for to in range(4) for other in range(2)]
     greeted += [(2 * z + lo, 4 * (first_z + 4 * t) + j) for t in range(2) for j in range(4)]
     for rep, grp in greeted:
@@ -99,6 +100,19 @@
             beyond[way] if hops == 4 else ring[way], g,
         )
 
+    def last_copy(way, half, other):
+        rows, owner = rows_of(half), 1 - h if other else h
+        return remote(
+            sum_send.at[way, 0, rows, pl.ds(pl.multiple_of(owner * COLS, COLS), COLS)],
+            last_recv.at[way, other, rows], last_sems.at[0, way, half, other], last_sems.at[1, way, half, other],
+            across[way] if other else ring[way], g,
+        )
+
+    def raw_copy():
+        return remote(
+            grad_v.at[0, :, one(y, 1 - h)], raw_recv, raw_sems.at[0], raw_sems.at[1], partner, g
+        )
+
     def swap(offset):
         return remote(
             grad_v.at[1, :, one(at(offset), 1 - h)], swapped.at[offset % NY],
@@ -125,6 +139,7 @@
             start(rs_copy(way, 3, 0, half, True))
     for offset in (3, -3, 2, -2, 1, -1, 0):
         start(swap(offset))
+    start(raw_copy())
     swap(4).wait_recv()
     for way in range(2):
         one_send[way, 3, rows_of(way), :] = with_swapped(4, rows_of(way)).astype(BF16)
@@ -145,7 +160,11 @@
                     rs_copy(way, 4, 0, half, True).wait_recv()
                     summed = summed + sum_recv[way, 3, rows, :].astype(F32)
                 sum_send[way, hops - 1, rows, :] = summed.astype(BF16)
-                start(rs_copy(way, hops, 0, half))
+                if hops == 2:
+                    start(rs_copy(way, 2, 0, half))
+                else:
+                    for other in (1, 0):
+                        start(last_copy(way, half, other))
         for way in range(2):
             swap(hops if way == 0 else -hops).wait_recv()
         for half in range(2):
@@ -159,48 +178,36 @@
                 one_send[way, hops - 1, rows, :] = summed.astype(BF16)
                 start(rs_copy(way, hops, 1, half))
 
-    def cross(half):
+    raw_copy().wait_recv()
+    for half in range(2):
         rows = rows_of(half)
-        return remote(
-            cross_send.at[rows], cross_recv.at[rows], cross_sems.at[0, half], cross_sems.at[1, half], partner, g
-        )
-
-    for half in range(2):
-        for way in range(2):
-            rs_copy(way, 1, 0, half).wait_recv()
-        rows = rows_of(half)
-
-        def last(owner, rows=rows):
-            side = pl.ds(pl.multiple_of(owner * COLS, COLS), COLS)
-            summed = grad_v[0, rows, one(y, owner)].astype(F32)
+        summed = grad_v[0, rows, one(y, h)].astype(F32) + raw_recv[rows, :].astype(F32)
+        for way in range(2):
+            for other in range(2):
+                last_copy(way, half, other).wait_recv()
+                summed = summed + last_recv[way, other, rows, :].astype(F32)
+        total[0, rows, :] = summed
+
+    def finish_one():
+        swap(0).wait_recv()
+        for half in range(2):
             for way in range(2):
-                summed = summed + sum_recv[way, 0, rows, side].astype(F32)
-            return summed
-
-        cross_send[rows, :] = last(1 - h).astype(BF16)
-        start(cross(half))
-        total[0, rows, :] = last(h)
-    swap(0).wait_recv()
-    for half in range(2):
-        for way in range(2):
-            rs_copy(way, 1, 1, half).wait_recv()
-        rows = rows_of(half)
-        summed = with_swapped(0, rows)
-        for way in range(2):
-            summed = summed + one_recv[way, 0, rows, :].astype(F32)
-        total[1, rows, :] = summed
+                rs_copy(way, 1, 1, half).wait_recv()
+            rows = rows_of(half)
+            summed = with_swapped(0, rows)
+            for way in range(2):
+                summed = summed + one_recv[way, 0, rows, :].astype(F32)
+            total[1, rows, :] = summed
 
     for load in loads:
         load.wait()
     slot = (z // 4) * 4 + g % 4
     shift = pl.multiple_of((g % 4) * 32, 32)
     stores = []
-    for layer in (1, 0):
+    for layer in range(LAYERS):
+        if layer == 1:
+            finish_one()
         gradient = total[layer]
-        if layer == 0:
-            for half in range(2):
-                cross(half).wait_recv()
-            gradient = gradient + cross_recv[...].astype(F32)
         moment = 0.9 * first_v[layer] + 0.1 * gradient
         square = 0.999 * second_v[layer] + 0.001 * gradient * gradient
         weight = master_v[layer]
@@ -235,11 +242,12 @@
         owner = 1 - h if other else h
         held = 2 if hops == 4 else hops - 1
         place = region(at(-held if way == 0 else held), owner, layer, way if hops == 4 else None)
-        source = piece.at[layer] if hops == 1 and not other else place
-        return remote(
-            source, place,
+        if hops == 1:
+            place = region(y, h, layer)
+        return remote(
+            piece.at[layer] if hops == 1 else place, place,
             ag_send.at[way, hops - 1, layer, other], ag_recv.at[way, hops - 1, layer, other],
-            beyond[way] if hops == 4 else ring[way], g,
+            beyond[way] if hops == 4 else across[way] if hops == 1 and other else ring[way], g,
         )
 
     def ag_cross_copy(layer):
@@ -247,7 +255,7 @@
             piece.at[layer], region(y, h, layer), ag_cross.at[0, layer], ag_cross.at[1, layer], partner, g
         )
 
-    for layer in (1, 0):
+    for layer in range(LAYERS):
         pltpu.make_async_copy(delta_recv.at[layer], delta_recv.at[layer], move_recv.at[layer]).wait()
         for t in range(2):
             low = [delta_recv[layer, 4 * t + j, :, :128].astype(F32) for j in range(4)]
@@ -258,9 +266,9 @@
                 piece[layer, t, :, place] = (actor_v[t, layer, :, place].astype(F32) + tile).astype(BF16)
         for way in range(2):
             start(ag_copy(way, 1, layer, 0))
-        if layer == 0:
-            start(ag_cross_copy(0))
-            start(ag_cross_copy(1))
+            if layer == 0:
+                start(ag_copy(way, 1, 0, 1))
+        start(ag_cross_copy(layer))
         store = pltpu.make_async_copy(piece.at[layer], region(y, h, layer), piece_sem.at[layer])
         store.start()
         stores.append(store)
@@ -272,10 +280,7 @@
     def gather(hops, layer, other, last=False):
         for way in range(2):
             for come in (3, 4) if last else (hops,):
-                if come == 0:
-                    ag_cross_copy(layer).wait_recv() if way == 0 else None
-                else:
-                    ag_copy(way, come, layer, other).wait_recv()
+                ag_copy(way, come, layer, other).wait_recv()
                 if come == 2:
                     start(ag_copy(way, 4, layer, other))
                 if come < 3:
@@ -283,17 +288,17 @@
                 if layer == 1:
                     start(over(come, way, 0))
 
+    gather(1, 0, 0)
     gather(1, 1, 0)
-    gather(1, 0, 0)
-    gather(0, 0, 1)
+    gather(1, 0, 1)
     gather(2, 1, 0)
     gather(2, 0, 0)
-    gather(1, 0, 1)
+    gather(2, 0, 1)
     gather(3, 1, 0, True)
-    gather(2, 0, 1)
     gather(3, 0, 0, True)
     gather(3, 0, 1, True)
-    ag_cross_copy(1).wait_recv()
+    for layer in range(LAYERS):
+        ag_cross_copy(layer).wait_recv()
     for hops in (1, 2, 3, 4):
         for way in range(2):
             over(hops, way, 1).wait_recv()
@@ -341,12 +346,12 @@
             pltpu.VMEM((2, LAYERS, PIECE, SPAN), BF16),
             pltpu.VMEM((2, 4, ROWS, 2 * COLS), BF16),
             pltpu.VMEM((2, 2, ROWS, 2 * COLS), BF16),
+            pltpu.VMEM((2, 2, ROWS, COLS), BF16),
+            pltpu.VMEM((ROWS, COLS), BF16),
             pltpu.VMEM((2, 4, ROWS, COLS), BF16),
             pltpu.VMEM((2, 4, ROWS, COLS), BF16),
             pltpu.VMEM((NY, ROWS, COLS), BF16),
             state_v,
-            pltpu.VMEM((ROWS, COLS), BF16),
-            pltpu.VMEM((ROWS, COLS), BF16),
             pltpu.VMEM((LAYERS, 256, COLS), F32),
             pltpu.VMEM((LAYERS, COLS, 256), BF16),
             pltpu.VMEM((LAYERS, 8, PIECE, 256), BF16),
@@ -355,8 +360,9 @@
             dma((3, LAYERS)),
             dma((2, 4, LAYERS, 2)),
             dma((2, 4, LAYERS, 2)),
+            dma((2, 2, 2, 2)),
+            dma((2,)),
             dma((2, NY)),
-            dma((2, 2)),
             dma((LAYERS, 4, 2)),
             dma((LAYERS,)),
             dma((2, 4, LAYERS, 2)),

time: 60.7 us -> 59.8 us (0.985); the launches traced: 59.6 us -> 59.7 us
  no operation moved by 1% of the time
where the time goes in v2:
time: 59.8 us; the launch traced here: 59.7 us
  Pallas kernels  59.1 us (99%)
  between operations  0.64 us (1%)
    pallas_call x1, Pallas kernels, body(): pl.pallas_call(kernel, out_shape=(jax.ShapeDtypeStruct((LAYERS, NY, 64, S...  57.8 us
    pallas_call x1, Pallas kernels, body(): pl.pallas_call(place_kernel, out_shape=(jax.ShapeDtypeStruct(actor_weight...  1.31 us

profile of v2, /device:TPU:6, one launch (start us, length us, event | category | flops | bytes accessed | tf_op | source)
XLA Modules:
  0.0 59.7 jit_solution(3123204895143538351)
XLA Ops:
  0.6 57.8 %shard_map.84 = (bf16[2,8,64,640]{3,2,1,0:T(8,128)(2,1)S(1)}, f32[2,160,128]{2,1,0:T(8,128)S(1)}, f32[2,160,128]{2,1,0:T(8,128)S(1)}, f32[2,160,128]{2,1,0:T(8,128)S(1)}) custom-call(bf16[1,2,160,2048]{3,2,1,0:T(8,128)(2,1)} %grad.1, f32[2,160,128]{2,1,0:T(8,128)} %master.1, f32[2,160,128]{2,1,0:T(8,128)} %first.1, f32[2,160,128]{2,1,0:T(8,128)} %second.1, ...), custom_call_target="tpu_custom_call" | custom-call | tf_op jit(solution)/shard_map/pallas_call | solution.py:336
  58.4 1.3 %shard_map.85 = (bf16[2,64,5120]{2,1,0:T(8,128)(2,1)}, f32[2,160,128]{2,1,0:T(8,128)}, f32[2,160,128]{2,1,0:T(8,128)}, f32[2,160,128]{2,1,0:T(8,128)}) custom-call(bf16[2,8,64,640]{3,2,1,0:T(8,128)(2,1)S(1)} %get-tuple-element.8.actor, f32[2,160,128]{2,1,0:T(8,128)S(1)} %get-tuple-element.9.master, f32[2,160,128]{2,1,0:T(8,128)S(1)} %get-tuple-element.10.first, ...), custom_call_target="tpu_custom_call" | custom-call | tf_op jit(solution)/shard_map/pallas_call | solution.py:378

commit v3 on v2

--- a/solution.py
+++ b/solution.py
@@ -38,6 +38,7 @@
     ring = (((y + 1) % NY) * 2 + h, ((y + NY - 1) % NY) * 2 + h)
     beyond = (((y + 2) % NY) * 2 + h, ((y + NY - 2) % NY) * 2 + h)
     across = (((y + 1) % NY) * 2 + 1 - h, ((y + NY - 1) % NY) * 2 + 1 - h)
+    far = (((y + 2) % NY) * 2 + 1 - h, ((y + NY - 2) % NY) * 2 + 1 - h)
     partner = y * 2 + (1 - h)
 
     def at(dy):
@@ -71,7 +72,7 @@
         return (2 * to + 1 - z % 2) * 2 + flip((z // 2) % 2, other), 2 * r + other
 
     barrier = pltpu.get_barrier_semaphore()
-    greeted = [(peer, g) for peer in (*ring, *beyond, *across, partner)]
+    greeted = [(peer, g) for peer in (*ring, *beyond, *across, *far, partner)]
     greeted += [target(to, other) for to in range(4) for other in range(2)]
     greeted += [(2 * z + lo, 4 * (first_z + 4 * t) + j) for t in range(2) for j in range(4)]
     for rep, grp in greeted:
@@ -239,15 +240,15 @@
         return new_actor.at[layer, z_range, pl.ds(pl.multiple_of((origin // 2) * PIECE, PIECE), PIECE)]
 
     def ag_copy(way, hops, layer, other):
-        owner = 1 - h if other else h
         held = 2 if hops == 4 else hops - 1
+        goes_across = other and hops in ((1,), (3, 4))[layer]
+        owner = 1 - h if other and not goes_across else h
         place = region(at(-held if way == 0 else held), owner, layer, way if hops == 4 else None)
-        if hops == 1:
-            place = region(y, h, layer)
+        near = across if goes_across else ring
         return remote(
             piece.at[layer] if hops == 1 else place, place,
             ag_send.at[way, hops - 1, layer, other], ag_recv.at[way, hops - 1, layer, other],
-            beyond[way] if hops == 4 else across[way] if hops == 1 and other else ring[way], g,
+            (far if goes_across else beyond)[way] if hops == 4 else near[way], g,
         )
 
     def ag_cross_copy(layer):
@@ -274,19 +275,18 @@
         stores.append(store)
 
     def over(hops, way, other):
-        place = region(at(-hops if way == 0 else hops), 1 - h if other else h, 1, way if hops == 4 else None)
+        place = region(at(-hops if way == 0 else hops), 1 - h if other else h, 1)
         return remote(place, place, ag_over.at[0, way, hops - 1], ag_over.at[1, way, hops - 1], partner, g)
 
-    def gather(hops, layer, other, last=False):
+    def gather(come, layer, other):
         for way in range(2):
-            for come in (3, 4) if last else (hops,):
-                ag_copy(way, come, layer, other).wait_recv()
-                if come == 2:
-                    start(ag_copy(way, 4, layer, other))
-                if come < 3:
-                    start(ag_copy(way, come + 1, layer, other))
-                if layer == 1:
-                    start(over(come, way, 0))
+            ag_copy(way, come, layer, other).wait_recv()
+            for to in (4, 3) if come == 2 else (2,):
+                start(ag_copy(way, to, layer, other))
+                if layer == 1 and come == 2:
+                    start(ag_copy(way, to, 1, 1))
+            if layer == 1:
+                start(over(come, way, 0))
 
     gather(1, 0, 0)
     gather(1, 1, 0)
@@ -294,14 +294,15 @@
     gather(2, 1, 0)
     gather(2, 0, 0)
     gather(2, 0, 1)
-    gather(3, 1, 0, True)
-    gather(3, 0, 0, True)
-    gather(3, 0, 1, True)
     for layer in range(LAYERS):
         ag_cross_copy(layer).wait_recv()
-    for hops in (1, 2, 3, 4):
-        for way in range(2):
+    for way in range(2):
+        for hops in (1, 2):
             over(hops, way, 1).wait_recv()
+        for hops in (3, 4):
+            for layer in range(LAYERS):
+                for other in range(2):
+                    ag_copy(way, hops, layer, other).wait_recv()
 
     for copy in sent:
         copy.wait_send()
@@ -368,7 +369,7 @@
             dma((2, 4, LAYERS, 2)),
             dma((2, 4, LAYERS, 2)),
             dma((2, LAYERS)),
-            dma((2, 2, 4)),
+            dma((2, 2, 2)),
             dma((LAYERS,)),
         ],
         compiler_params=pltpu.CompilerParams(

time: 59.8 us -> 58.9 us (0.985); the launches traced: 59.7 us -> 57.7 us
  Pallas kernels: 59.1 us -> 57.1 us
    pallas_call x1, Pallas kernels: 57.8 us -> 55.8 us  [body(): pl.pallas_call(kernel, out_shape=(jax.ShapeDtypeStruct((LAYERS, NY, 64, S...]
where the time goes in v3:
time: 58.9 us; the launch traced here: 57.7 us
  Pallas kernels  57.1 us (97%)
  between operations  0.64 us (1%)
    pallas_call x1, Pallas kernels, body(): pl.pallas_call(kernel, out_shape=(jax.ShapeDtypeStruct((LAYERS, NY, 64, S...  55.8 us
    pallas_call x1, Pallas kernels, body(): pl.pallas_call(place_kernel, out_shape=(jax.ShapeDtypeStruct(actor_weight...  1.31 us

profile of v3, /device:TPU:6, one launch (start us, length us, event | category | flops | bytes accessed | tf_op | source)
XLA Modules:
  0.0 57.7 jit_solution(7574571650272573175)
XLA Ops:
  0.6 55.8 %shard_map.84 = (bf16[2,8,64,640]{3,2,1,0:T(8,128)(2,1)S(1)}, f32[2,160,128]{2,1,0:T(8,128)S(1)}, f32[2,160,128]{2,1,0:T(8,128)S(1)}, f32[2,160,128]{2,1,0:T(8,128)S(1)}) custom-call(bf16[1,2,160,2048]{3,2,1,0:T(8,128)(2,1)} %grad.1, f32[2,160,128]{2,1,0:T(8,128)} %master.1, f32[2,160,128]{2,1,0:T(8,128)} %first.1, f32[2,160,128]{2,1,0:T(8,128)} %second.1, ...), custom_call_target="tpu_custom_call" | custom-call | tf_op jit(solution)/shard_map/pallas_call | solution.py:337
  56.4 1.3 %shard_map.85 = (bf16[2,64,5120]{2,1,0:T(8,128)(2,1)}, f32[2,160,128]{2,1,0:T(8,128)}, f32[2,160,128]{2,1,0:T(8,128)}, f32[2,160,128]{2,1,0:T(8,128)}) custom-call(bf16[2,8,64,640]{3,2,1,0:T(8,128)(2,1)S(1)} %get-tuple-element.8.actor, f32[2,160,128]{2,1,0:T(8,128)S(1)} %get-tuple-element.9.master, f32[2,160,128]{2,1,0:T(8,128)S(1)} %get-tuple-element.10.first, ...), custom_call_target="tpu_custom_call" | custom-call | tf_op jit(solution)/shard_map/pallas_call | solution.py:379

commit v4 on v3

--- a/solution.py
+++ b/solution.py
@@ -133,12 +133,13 @@
         return grad_v[1, rows, one(at(offset), h)].astype(F32) + swapped[offset % NY, rows, :].astype(F32)
 
     grad_load.wait()
-    start(swap(4))
+    for offset in (4, 3, -3):
+        start(swap(offset))
     for half in range(2):
         start(rs_copy(half, 4, 0, half, True))
         for way in range(2):
             start(rs_copy(way, 3, 0, half, True))
-    for offset in (3, -3, 2, -2, 1, -1, 0):
+    for offset in (2, -2, 1, -1, 0):
         start(swap(offset))
     start(raw_copy())
     swap(4).wait_recv()
@@ -274,35 +275,53 @@
         store.start()
         stores.append(store)
 
+    def both_copy(way, hops):
+        held = 2 if hops == 4 else hops - 1
+        origin = at(-held if way == 0 else held)
+        z_block = (1 - origin % 2) * 4
+        z_range = pl.ds(z_block + 2 * way, 2) if hops == 4 else pl.ds(z_block, 4)
+        place = new_actor.at[0, z_range, pl.ds(pl.multiple_of((origin // 2) * PIECE, PIECE), PIECE)]
+        return remote(
+            place, place, ag_send.at[way, hops - 1, 0, 0], ag_recv.at[way, hops - 1, 0, 0],
+            (beyond if hops == 4 else ring)[way], g,
+        )
+
+    def gather_both(come):
+        for way in range(2):
+            if come == 1:
+                for other in range(2):
+                    ag_copy(way, 1, 0, other).wait_recv()
+            else:
+                both_copy(way, come).wait_recv()
+            for to in (4, 3) if come == 2 else (2,):
+                start(both_copy(way, to))
+
     def over(hops, way, other):
         place = region(at(-hops if way == 0 else hops), 1 - h if other else h, 1)
         return remote(place, place, ag_over.at[0, way, hops - 1], ag_over.at[1, way, hops - 1], partner, g)
 
-    def gather(come, layer, other):
-        for way in range(2):
-            ag_copy(way, come, layer, other).wait_recv()
+    def gather_one(come):
+        for way in range(2):
+            ag_copy(way, come, 1, 0).wait_recv()
             for to in (4, 3) if come == 2 else (2,):
-                start(ag_copy(way, to, layer, other))
-                if layer == 1 and come == 2:
+                start(ag_copy(way, to, 1, 0))
+                if come == 2:
                     start(ag_copy(way, to, 1, 1))
-            if layer == 1:
-                start(over(come, way, 0))
-
-    gather(1, 0, 0)
-    gather(1, 1, 0)
-    gather(1, 0, 1)
-    gather(2, 1, 0)
-    gather(2, 0, 0)
-    gather(2, 0, 1)
+            start(over(come, way, 0))
+
+    gather_both(1)
+    gather_one(1)
+    gather_both(2)
+    gather_one(2)
     for layer in range(LAYERS):
         ag_cross_copy(layer).wait_recv()
     for way in range(2):
         for hops in (1, 2):
             over(hops, way, 1).wait_recv()
         for hops in (3, 4):
-            for layer in range(LAYERS):
-                for other in range(2):
-                    ag_copy(way, hops, layer, other).wait_recv()
+            both_copy(way, hops).wait_recv()
+            for other in range(2):
+                ag_copy(way, hops, 1, other).wait_recv()
 
     for copy in sent:
         copy.wait_send()

time: 58.9 us -> 61.4 us (1.042)
  the two profiles are of different devices: /device:TPU:6 before, /device:TPU:2 now
where the time goes in v4:
time: 61.4 us; the launch traced here: 61.3 us
  Pallas kernels  60.7 us (99%)
  between operations  0.64 us (1%)
    pallas_call x1, Pallas kernels, body(): pl.pallas_call(kernel, out_shape=(jax.ShapeDtypeStruct((LAYERS, NY, 64, S...  59.3 us
    pallas_call x1, Pallas kernels, body(): pl.pallas_call(place_kernel, out_shape=(jax.ShapeDtypeStruct(actor_weight...  1.31 us

profile of v4, /device:TPU:2, one launch (start us, length us, event | category | flops | bytes accessed | tf_op | source)
XLA Modules:
  0.0 61.3 jit_solution(3175567928688455750)
XLA Ops:
  0.6 59.3 %shard_map.84 = (bf16[2,8,64,640]{3,2,1,0:T(8,128)(2,1)S(1)}, f32[2,160,128]{2,1,0:T(8,128)S(1)}, f32[2,160,128]{2,1,0:T(8,128)S(1)}, f32[2,160,128]{2,1,0:T(8,128)S(1)}) custom-call(bf16[1,2,160,2048]{3,2,1,0:T(8,128)(2,1)} %grad.1, f32[2,160,128]{2,1,0:T(8,128)} %master.1, f32[2,160,128]{2,1,0:T(8,128)} %first.1, f32[2,160,128]{2,1,0:T(8,128)} %second.1, ...), custom_call_target="tpu_custom_call" | custom-call | tf_op jit(solution)/shard_map/pallas_call | solution.py:356
  60.0 1.3 %shard_map.85 = (bf16[2,64,5120]{2,1,0:T(8,128)(2,1)}, f32[2,160,128]{2,1,0:T(8,128)}, f32[2,160,128]{2,1,0:T(8,128)}, f32[2,160,128]{2,1,0:T(8,128)}) custom-call(bf16[2,8,64,640]{3,2,1,0:T(8,128)(2,1)S(1)} %get-tuple-element.8.actor, f32[2,160,128]{2,1,0:T(8,128)S(1)} %get-tuple-element.9.master, f32[2,160,128]{2,1,0:T(8,128)S(1)} %get-tuple-element.10.first, ...), custom_call_target="tpu_custom_call" | custom-call | tf_op jit(solution)/shard_map/pallas_call | solution.py:398

commit v5 on v3

--- a/solution.py
+++ b/solution.py
@@ -239,15 +239,15 @@
         z_range = pl.ds(z_block, 2) if half is None else pl.ds(z_block + half, 1)
         return new_actor.at[layer, z_range, pl.ds(pl.multiple_of((origin // 2) * PIECE, PIECE), PIECE)]
 
-    def ag_copy(way, hops, layer, other):
+    def ag_copy(way, hops, layer, other, t):
         held = 2 if hops == 4 else hops - 1
         goes_across = other and hops in ((1,), (3, 4))[layer]
         owner = 1 - h if other and not goes_across else h
-        place = region(at(-held if way == 0 else held), owner, layer, way if hops == 4 else None)
+        place = region(at(-held if way == 0 else held), owner, layer, t)
         near = across if goes_across else ring
         return remote(
-            piece.at[layer] if hops == 1 else place, place,
-            ag_send.at[way, hops - 1, layer, other], ag_recv.at[way, hops - 1, layer, other],
+            piece.at[layer, pl.ds(t, 1)] if hops == 1 else place, place,
+            ag_send.at[way, hops - 1, layer, other, t], ag_recv.at[way, hops - 1, layer, other, t],
             (far if goes_across else beyond)[way] if hops == 4 else near[way], g,
         )
 
@@ -265,10 +265,10 @@
             for index, tile in enumerate(tiles):
                 place = slice(index * 128, index * 128 + 128)
                 piece[layer, t, :, place] = (actor_v[t, layer, :, place].astype(F32) + tile).astype(BF16)
-        for way in range(2):
-            start(ag_copy(way, 1, layer, 0))
-            if layer == 0:
-                start(ag_copy(way, 1, 0, 1))
+            for way in range(2):
+                start(ag_copy(way, 1, layer, 0, t))
+                if layer == 0:
+                    start(ag_copy(way, 1, 0, 1, t))
         start(ag_cross_copy(layer))
         store = pltpu.make_async_copy(piece.at[layer], region(y, h, layer), piece_sem.at[layer])
         store.start()
@@ -279,13 +279,16 @@
         return remote(place, place, ag_over.at[0, way, hops - 1], ag_over.at[1, way, hops - 1], partner, g)
 
     def gather(come, layer, other):
-        for way in range(2):
-            ag_copy(way, come, layer, other).wait_recv()
-            for to in (4, 3) if come == 2 else (2,):
-                start(ag_copy(way, to, layer, other))
-                if layer == 1 and come == 2:
-                    start(ag_copy(way, to, 1, 1))
-            if layer == 1:
+        for t in range(2):
+            for way in range(2):
+                ag_copy(way, come, layer, other, t).wait_recv()
+                for to in (4, 3) if come == 2 else (2,):
+                    if to < 4 or t == way:
+                        start(ag_copy(way, to, layer, other, t))
+                        if layer == 1 and come == 2:
+                            start(ag_copy(way, to, 1, 1, t))
+        if layer == 1:
+            for way in range(2):
                 start(over(come, way, 0))
 
     gather(1, 0, 0)
@@ -302,7 +305,8 @@
         for hops in (3, 4):
             for layer in range(LAYERS):
                 for other in range(2):
-                    ag_copy(way, hops, layer, other).wait_recv()
+                    for t in range(2) if hops == 3 else (way,):
+                        ag_copy(way, hops, layer, other, t).wait_recv()
 
     for copy in sent:
         copy.wait_send()
@@ -366,8 +370,8 @@
             dma((2, NY)),
             dma((LAYERS, 4, 2)),
             dma((LAYERS,)),
-            dma((2, 4, LAYERS, 2)),
-            dma((2, 4, LAYERS, 2)),
+            dma((2, 4, LAYERS, 2, 2)),
+            dma((2, 4, LAYERS, 2, 2)),
             dma((2, LAYERS)),
             dma((2, 2, 2)),
             dma((LAYERS,)),

time: 58.9 us -> 59.4 us (level)
  the two profiles are of different devices: /device:TPU:6 before, /device:TPU:2 now
where the time goes in v5:
time: 59.4 us; the launch traced here: 59.2 us
  Pallas kernels  58.6 us (99%)
  between operations  0.64 us (1%)
    pallas_call x1, Pallas kernels, body(): pl.pallas_call(kernel, out_shape=(jax.ShapeDtypeStruct((LAYERS, NY, 64, S...  57.3 us
    pallas_call x1, Pallas kernels, body(): pl.pallas_call(place_kernel, out_shape=(jax.ShapeDtypeStruct(actor_weight...  1.31 us

profile of v5, /device:TPU:2, one launch (start us, length us, event | category | flops | bytes accessed | tf_op | source)
XLA Modules:
  0.0 59.2 jit_solution(17677026091399846508)
XLA Ops:
  0.6 57.3 %shard_map.84 = (bf16[2,8,64,640]{3,2,1,0:T(8,128)(2,1)S(1)}, f32[2,160,128]{2,1,0:T(8,128)S(1)}, f32[2,160,128]{2,1,0:T(8,128)S(1)}, f32[2,160,128]{2,1,0:T(8,128)S(1)}) custom-call(bf16[1,2,160,2048]{3,2,1,0:T(8,128)(2,1)} %grad.1, f32[2,160,128]{2,1,0:T(8,128)} %master.1, f32[2,160,128]{2,1,0:T(8,128)} %first.1, f32[2,160,128]{2,1,0:T(8,128)} %second.1, ...), custom_call_target="tpu_custom_call" | custom-call | tf_op jit(solution)/shard_map/pallas_call | solution.py:341
  57.9 1.3 %shard_map.85 = (bf16[2,64,5120]{2,1,0:T(8,128)(2,1)}, f32[2,160,128]{2,1,0:T(8,128)}, f32[2,160,128]{2,1,0:T(8,128)}, f32[2,160,128]{2,1,0:T(8,128)}) custom-call(bf16[2,8,64,640]{3,2,1,0:T(8,128)(2,1)S(1)} %get-tuple-element.8.actor, f32[2,160,128]{2,1,0:T(8,128)S(1)} %get-tuple-element.9.master, f32[2,160,128]{2,1,0:T(8,128)S(1)} %get-tuple-element.10.first, ...), custom_call_target="tpu_custom_call" | custom-call | tf_op jit(solution)/shard_map/pallas_call | solution.py:383
